TPU v7x, 256 devices: a whole 4x4x8 slice. The times are simulated.
256 devices in a mesh: expert: 32 (over y, x, core), tensor: 8 (over z).
Axes of the slice: x: 4, y: 4, z: 8, core: 2. Of those that a mesh axis runs over, the one named last changes fastest.
Arguments:
- tokens: bfloat16 [16384, 4096], P('expert', 'tensor'), may hold values from -36 to 36
- expert_ids: int32 [16384, 1], P('expert'), may hold values from 0 to 63; in each aligned block of 512 rows (0 to 511, 512 to 1023, ...) at most 16 rows name the same one
- gates: float32 [16384, 1], P('expert'), may hold values from 0.25 to 1
- expert_in: bfloat16 [64, 4096, 2048], P('expert', 'tensor'), may hold values from -0.09375 to 0.09375
- expert_out: bfloat16 [64, 2048, 4096], P('expert', None, 'tensor'), may hold values from -0.125 to 0.125
- norm_gain: float32 [4096], replicated, may hold values from 0.5 to 2
- up_weight: bfloat16 [4096, 8192], P('expert', 'tensor'), may hold values from -0.09375 to 0.09375
- down_weight: bfloat16 [4096, 8192], P('expert', 'tensor'), may hold values from -0.0625 to 0.0625
Outputs:
- layer_output: bfloat16 [16384, 4096], P('expert', 'tensor')
Inputs may be any that keep to these rules, and one draw needn't show every extreme that they name: `expert_ids`: among the 512 tokens of one block, at most 16 carry the same expert id; in some blocks one id is carried by exactly 16 tokens.
All inputs are finite; a program needn't handle non-finite values.
Results may differ from a plain program's by a relative error of at most 0.015.
Values may be sent and summed in bfloat16 or wider, within the bound.
No kernel may reach another device: no remote copies, remote signals or barrier semaphores. Data moves between devices by JAX's collectives and lax.ppermute only.
A program may use at most 128 MiB of HBM per device.

v0:
```python
import jax
import jax.numpy as jnp
from jax import lax
from jax.sharding import PartitionSpec as P

EXP_DEV = 2


def slot_table(expert_col, experts, capacity):
    expert = expert_col[:, 0]
    count = expert.shape[0]
    order = jnp.arange(count, dtype=jnp.int32)
    same = (expert[:, None] == expert[None, :]) & (order[None, :] < order[:, None])
    position = jnp.sum(same.astype(jnp.int32), axis=1)
    slot_index = expert * capacity + position
    selector = jnp.arange(experts * capacity, dtype=jnp.int32)[:, None] == slot_index[None, :]
    return selector.astype(jnp.bfloat16)


def trade(buffer):
    result = lax.all_to_all(buffer, "expert", split_axis=0, concat_axis=0, tiled=True)
    return result


def gather_rows(weight, combine, start_value):
    return combine(start_value, lax.all_gather(weight, "expert", axis=0, tiled=True), jnp.int32(0))


def shards(tokens, expert_ids, gates, expert_in, expert_out, norm_gain, up_weight, down_weight):
    token_count = tokens.shape[0]
    local_width = tokens.shape[1]
    groups = lax.axis_size("expert")
    experts = EXP_DEV * groups
    capacity = 2 * token_count // experts
    selector = slot_table(expert_ids, experts, capacity)
    outgoing = jnp.dot(selector, tokens, preferred_element_type=jnp.float32).astype(jnp.bfloat16)
    outgoing = outgoing.reshape(groups, EXP_DEV, capacity, local_width)
    arrived = trade(outgoing)
    partial_value = jnp.einsum(
        "sjcd,jdh->sjch", arrived, expert_in, preferred_element_type=jnp.float32
    )
    summed = lax.psum(partial_value.astype(jnp.bfloat16), "tensor").astype(jnp.float32)
    active = jax.nn.relu(summed).astype(jnp.bfloat16)
    produced = jnp.einsum(
        "sjch,jhd->sjcd", active, expert_out, preferred_element_type=jnp.float32
    ).astype(jnp.bfloat16)
    returned = trade(produced).reshape(experts * capacity, local_width)
    routed = lax.dot_general(
        selector, returned, (((0,), (0,)), ((), ())), preferred_element_type=jnp.float32
    )
    mixed = (tokens.astype(jnp.float32) + gates * routed).astype(jnp.bfloat16)
    whole = lax.all_gather(mixed, "tensor", axis=1, tiled=True)
    whole_f32 = whole.astype(jnp.float32)
    mean_square = jnp.mean(whole_f32 * whole_f32, axis=1, keepdims=True)
    normed = (whole_f32 * lax.rsqrt(mean_square + 1e-06) * norm_gain).astype(jnp.bfloat16)

    def add_up(carry, piece, start):
        return jnp.dot(normed, piece, preferred_element_type=jnp.float32)

    ffn_hidden = gather_rows(
        up_weight, add_up, jnp.zeros((token_count, up_weight.shape[1]), jnp.float32)
    )
    ffn_active = jax.nn.gelu(ffn_hidden, approximate=True).astype(jnp.bfloat16)

    def add_down(carry, piece, start):
        contribution = lax.dot_general(
            ffn_active, piece, (((1,), (1,)), ((), ())), preferred_element_type=jnp.float32
        )
        return contribution

    outputs = gather_rows(
        down_weight, add_down, jnp.zeros((token_count, whole.shape[1]), jnp.float32)
    )
    summed_out = lax.psum_scatter(
        outputs.astype(jnp.bfloat16), "tensor", scatter_dimension=1, tiled=True
    ).astype(jnp.float32)
    return (mixed.astype(jnp.float32) + summed_out).astype(jnp.bfloat16)


def solution(mesh):
    return jax.shard_map(
        shards,
        mesh=mesh,
        in_specs=(
            P("expert", "tensor"),
            P("expert", None),
            P("expert", None),
            P("expert", "tensor", None),
            P("expert", None, "tensor"),
            P(),
            P("expert", "tensor"),
            P("expert", "tensor"),
        ),
        out_specs=P("expert", "tensor"),
        check_vma=False,
    )
```

profile of v0, /device:TPU:1, one launch (start us, length us, event | category | flops | bytes accessed | tf_op | source)
XLA Modules:
  0.0 422.7 jit_solution(1282529528484603267)
XLA Ops:
  6.5 0.0 all-reduce.2.cloned.1.call-start
  6.5 0.0 copy-start.1
  6.5 1.1 convert_reduce_fusion
  7.6 0.9 multiply_add_fusion
  8.5 1.8 fusion.24
  10.3 25.6 %all_to_all.10 = bf16[32,2,16,512]{3,2,1,0:T(8,128)(2,1)S(1)} all-to-all(bf16[32,2,16,512]{3,2,1,0:T(8,128)(2,1)S(1)} %bitcast.30), channel_id=1, replica_groups=mesh['expert'=32,'tensor'=8] {'expert'}, dimensions={0} | all-to-all | bytes 2097152 | tf_op jit(solution)/shard_map/all_to_all | solution.py:21
  35.8 0.0 copy-done.1
  35.8 4.3 %convert_bitcast_fusion = bf16[32,2,16,2048]{3,2,0,1:T(8,128)(2,1)} fusion(bf16[2,512,2048]{2,1,0:T(8,128)(2,1)S(1)} %copy-done.1, bf16[32,2,16,512]{3,2,1,0:T(8,128)(2,1)S(1)} %all_to_all.10), kind=kOutput, calls=%fused_computation.15 | convolution fusion | flops 2149580800 | bytes 9437184 | tf_op jit(solution)/shard_map/sjcd,jdh->sjch/dot_general | solution.py:39
  40.2 0.0 all-reduce.2.cloned.1.call-update
  40.2 0.0 all-gather.4.cloned.1.call-start
  40.2 108.1 %all-reduce.2.cloned.1.call-done = bf16[32,2,16,2048]{3,2,0,1:T(8,128)(2,1)} async-done(((bf16[32,2,16,2048]{3,2,0,1:T(8,128)(2,1)}), bf16[32,2,16,2048]{3,2,0,1:T(8,128)(2,1)}) %all-reduce.2.cloned.1.call-update) | async-done | bytes 4194320 | tf_op jit(solution)/shard_map/psum | solution.py:42
  148.3 5.8 %fusion.30 = bf16[32,2,16,512]{3,2,0,1:T(8,128)(2,1)S(1)} fusion(bf16[2,2048,512]{2,1,0:T(8,128)(2,1)} %param.12, bf16[32,2,16,2048]{3,2,0,1:T(8,128)(2,1)} %all-reduce.2.cloned.1.call-done), kind=kOutput, calls=%fused_computation.30 | convolution fusion | flops 2154299392 | bytes 9437184 | tf_op jit(solution)/shard_map/sjch,jhd->sjcd/dot_general | solution.py:44
  154.1 0.0 copy-start.2
  154.1 0.0 copy-start.4
  154.1 0.1 copy.15
  154.2 24.6 %all_to_all.11 = bf16[32,2,16,512]{3,2,1,0:T(8,128)(2,1)S(1)} all-to-all(bf16[32,2,16,512]{3,2,1,0:T(8,128)(2,1)S(1)} %copy.15), channel_id=1, replica_groups=mesh['expert'=32,'tensor'=8] {'expert'}, dimensions={0} | all-to-all | bytes 2097152 | tf_op jit(solution)/shard_map/all_to_all | solution.py:21
  178.8 0.0 copy-done.2
  178.9 0.0 copy-done.4
  178.9 0.0 copy-start.3
  178.9 1.6 fusion.35
  180.4 0.0 all-gather.4.cloned.1.call-update
  180.5 0.0 all-gather.6.cloned.1.call-start
  180.5 0.7 all-gather.6.cloned.1.call-update
  181.2 0.0 all-gather.8.cloned.1.call-start
  181.2 0.5 all-gather.8.cloned.1.call-update
  181.8 0.2 reduce-scatter.2.cloned.1.call-start
  182.0 48.4 %all-gather.4.cloned.1.call-done = bf16[512,4096]{1,0:T(8,128)(2,1)} async-done(((bf16[512,512]{1,0:T(8,128)(2,1)}), bf16[512,4096]{1,0:T(8,128)(2,1)}) %all-gather.4.cloned.1.call-update) | async-done | bytes 4194320 | tf_op jit(solution)/shard_map/all_gather | solution.py:52
  230.4 3.1 fusion
  233.4 56.4 %all-gather.6.cloned.1.call-done = bf16[4096,1024]{1,0:T(8,128)(2,1)} async-done(((bf16[128,1024]{1,0:T(8,128)(2,1)}), bf16[4096,1024]{1,0:T(8,128)(2,1)}) %all-gather.6.cloned.1.call-update) | async-done | bytes 8388624 | tf_op jit(solution)/shard_map/all_gather | solution.py:26
  289.9 0.0 copy-done.3
  289.9 9.6 %fusion.21 = bf16[512,1024]{1,0:T(8,128)(2,1)S(1)} fusion(bf16[4096,1024]{1,0:T(8,128)(2,1)} %all-gather.6.cloned.1.call-done, bf16[512,4096]{1,0:T(8,128)(2,1)} %all-gather.4.cloned.1.call-done, f32[4096]{0:T(1024)S(1)} %copy-done.3, f32[512]{0:T(512)S(1)} %add_rsqrt_fusion), kind=kOutput, calls=%fused_computation.24 | convolution fusion | flops 4308074496 | bytes 13649920 | tf_op jit(solution)/shard_map/dot_general | solution.py:58
  299.5 50.4 %all-gather.8.cloned.1.call-done = bf16[4096,1024]{1,0:T(8,128)(2,1)} async-done(((bf16[128,1024]{1,0:T(8,128)(2,1)}), bf16[4096,1024]{1,0:T(8,128)(2,1)}) %all-gather.8.cloned.1.call-update) | async-done | bytes 8388624 | tf_op jit(solution)/shard_map/all_gather | solution.py:26
  349.9 9.6 %convolution_convert_fusion = bf16[512,4096]{1,0:T(8,128)(2,1)} fusion(bf16[512,1024]{1,0:T(8,128)(2,1)S(1)} %fusion.21, bf16[4096,1024]{1,0:T(8,128)(2,1)} %all-gather.8.cloned.1.call-done), kind=kOutput, calls=%fused_computation.6 | convolution fusion | flops 4297064448 | bytes 13631488 | tf_op jit(solution)/shard_map/dot_general | solution.py:66
  359.5 0.0 copy-start
  359.5 0.0 reduce-scatter.2.cloned.1.call-update
  359.5 54.7 %reduce-scatter.2.cloned.1.call-done = bf16[512,512]{1,0:T(8,128)(2,1)} async-done(((bf16[512,4096]{1,0:T(8,128)(2,1)}), bf16[512,512]{1,0:T(8,128)(2,1)}) %reduce-scatter.2.cloned.1.call-update) | async-done | bytes 524304 | tf_op jit(solution)/shard_map/reduce_scatter | solution.py:74
  414.2 0.0 copy-done
  414.2 2.0 add_convert_fusion
  (1 shorter events, 0.0 us)
Async XLA Ops:
  6.5 141.8 %all-reduce.2.cloned.1.call-start = ((), (), s32[]{:S(2)}) async-start(), calls=%async_computation.3 | async-start | bytes 8388608 | tf_op jit(solution)/shard_map/psum | solution.py:42
  6.5 29.3 %copy-start.1 = (bf16[2,512,2048]{2,1,0:T(8,128)(2,1)S(1)}, bf16[2,512,2048]{2,1,0:T(8,128)(2,1)}, u32[]{:S(2)}) copy-start(bf16[2,512,2048]{2,1,0:T(8,128)(2,1)} %param.11) | copy-start | bytes 12582916
  40.2 190.2 %all-gather.4.cloned.1.call-start = ((), (), s32[]{:S(2)}) async-start(), calls=%async_computation.4 | async-start | bytes 4718592 | tf_op jit(solution)/shard_map/all_gather | solution.py:52
  154.1 24.7 %copy-start.2 = (bf16[512,512]{1,0:T(8,128)(2,1)S(1)}, bf16[512,512]{1,0:T(8,128)(2,1)}, u32[]{:S(2)}) copy-start(bf16[512,512]{1,0:T(8,128)(2,1)} %param.8) | copy-start | bytes 1572868
  154.1 24.7 %copy-start.4 = (f32[512,1]{0,1:T(1,128)S(1)}, f32[512,1]{0,1:T(1,128)}, u32[]{:S(2)}) copy-start(f32[512,1]{0,1:T(1,128)} %param.10) | copy-start | bytes 6148
  178.9 111.0 %copy-start.3 = (f32[4096]{0:T(1024)S(1)}, f32[4096]{0:T(1024)}, u32[]{:S(2)}) copy-start(f32[4096]{0:T(1024)} %param.13) | copy-start | bytes 49156
  180.5 109.4 %all-gather.6.cloned.1.call-start = ((), (), s32[]{:S(2)}) async-start(), calls=%async_computation.5 | async-start | bytes 8650752 | tf_op jit(solution)/shard_map/all_gather | solution.py:26
  181.2 168.7 %all-gather.8.cloned.1.call-start = ((), (), s32[]{:S(2)}) async-start(), calls=%async_computation.6 | async-start | bytes 8650752 | tf_op jit(solution)/shard_map/all_gather | solution.py:26
  181.8 232.5 %reduce-scatter.2.cloned.1.call-start = ((), (), s32[]{:S(2)}) async-start(), calls=%async_computation.7 | async-start | bytes 4718592 | tf_op jit(solution)/shard_map/reduce_scatter | solution.py:74
  359.5 54.8 %copy-start = (bf16[512,512]{1,0:T(8,128)(2,1)S(1)}, bf16[512,512]{1,0:T(8,128)(2,1)}, u32[]{:S(2)}) copy-start(bf16[512,512]{1,0:T(8,128)(2,1)} %fusion.35) | copy-start | bytes 1572868
Sparse Core Ops, SparseCore 0:
  40.3 107.9 all-reduce.1
  180.6 49.7 all-gather.3
  232.9 56.9 all-gather.5
  292.3 57.5 all-gather.7
  359.6 54.5 reduce-scatter.1
where the time goes:
time: 423 us
  waiting for transfers between devices  319 us (75%)
  blocking collectives  50.2 us (12%)
  matrix products  32.6 us (8%)
  between operations  13.2 us (3%)
  other arithmetic  7.03 us (2%)
    psum x1, waiting for transfers between devices, shards(): lax.psum(partial_value.astype(jnp.bfloat16), 'tensor').astype(jnp.float32)  108 us
    all_gather x2, waiting for transfers between devices, gather_rows(): lax.all_gather(weight, 'expert', axis=0, tiled=True)  107 us
    reduce_scatter x1, waiting for transfers between devices, shards(): lax.psum_scatter(outputs.astype(jnp.bfloat16), 'tensor', scatter_dimensio...  54.7 us
    all_to_all x2, blocking collectives, trade(): lax.all_to_all(buffer, 'expert', split_axis=0, concat_axis=0, tiled=True)  50.2 us
    all_gather x1, waiting for transfers between devices, shards(): whole = lax.all_gather(mixed, 'tensor', axis=1, tiled=True)  48.4 us
    dot_general x1, matrix products, add_up(): return jnp.dot(normed, piece, preferred_element_type=jnp.float32)  9.58 us
    dot_general x1, matrix products, add_down(): lax.dot_general(ffn_active, piece, (((1,), (1,)), ((), ())), preferred_el...  9.57 us
  transfers between devices with their start and end apart: 5, of which 5 were waited for; matrix products, arithmetic and copies ran while one was open for 3% of the time, Pallas kernels for 0%

commit v1 on v0

--- a/solution.py
+++ b/solution.py
@@ -49,7 +49,14 @@
         selector, returned, (((0,), (0,)), ((), ())), preferred_element_type=jnp.float32
     )
     mixed = (tokens.astype(jnp.float32) + gates * routed).astype(jnp.bfloat16)
-    whole = lax.all_gather(mixed, "tensor", axis=1, tiled=True)
+    ring = [mixed]
+    for hop in range(7):
+        ring.append(lax.ppermute(ring[-1], "tensor", [(dev, (dev + 1) % 8) for dev in range(8)]))
+    whole = jnp.roll(
+        jnp.concatenate(ring[::-1], axis=1),
+        (lax.axis_index("tensor") + 1) * ring[0].shape[1],
+        axis=1,
+    )
     whole_f32 = whole.astype(jnp.float32)
     mean_square = jnp.mean(whole_f32 * whole_f32, axis=1, keepdims=True)
     normed = (whole_f32 * lax.rsqrt(mean_square + 1e-06) * norm_gain).astype(jnp.bfloat16)

time: 423 us -> 366 us (0.87)
  waiting for transfers between devices: 319 us -> 269 us
  blocking collectives: 50.2 us -> 25.6 us
  local copies, waits for them, and re-layouts: 0.09 us -> 10.2 us
  starting transfers between devices: 0.34 us -> 7.76 us
    all_gather x2, waiting for transfers between devices: 107 us -> 0.05 us  [gather_rows(): lax.all_gather(weight, 'expert', axis=0, tiled=True)]
    ppermute x0 -> x7, waiting for transfers between devices: none -> 83.5 us  [shards(): lax.ppermute(ring[-1], 'tensor', [(dev, (dev + 1) % 8) for dev in range(8)])]
    all_gather x1 -> x0, waiting for transfers between devices: 48.4 us -> none  [shards(): whole = lax.all_gather(mixed, 'tensor', axis=1, tiled=True)]
    all_to_all x2 -> x1, blocking collectives: 50.2 us -> 25.6 us  [trade(): lax.all_to_all(buffer, 'expert', split_axis=0, concat_axis=0, tiled=True)]
    all_to_all x0 -> x1, waiting for transfers between devices: none -> 16.9 us  [trade(): lax.all_to_all(buffer, 'expert', split_axis=0, concat_axis=0, tiled=True)]
    unnamed x10 -> x24, local copies, waits for them, and re-layouts: 0.02 us -> 8.16 us
    all_to_all x0 -> x1, starting transfers between devices: none -> 7.54 us  [trade(): lax.all_to_all(buffer, 'expert', split_axis=0, concat_axis=0, tiled=True)]
    reduce_scatter x1, waiting for transfers between devices: 54.7 us -> 60.2 us  [shards(): lax.psum_scatter(outputs.astype(jnp.bfloat16), 'tensor', scatter_dimensio...]
  transfers between devices with their start and end apart: 5 -> 12, of which waited for: 5 -> 10; matrix products, arithmetic and copies ran while one was open for 3% -> 6% of each run, Pallas kernels for 0% -> 0%
where the time goes in v1:
time: 366 us
  waiting for transfers between devices  269 us (73%)
  matrix products  34.4 us (9%)
  blocking collectives  25.6 us (7%)
  between operations  15.1 us (4%)
  local copies, waits for them, and re-layouts  10.2 us (3%)
  starting transfers between devices  7.76 us (2%)
  other arithmetic  3.82 us (1%)
    psum x1, waiting for transfers between devices, shards(): lax.psum(partial_value.astype(jnp.bfloat16), 'tensor').astype(jnp.float32)  107 us
    ppermute x7, waiting for transfers between devices, shards(): lax.ppermute(ring[-1], 'tensor', [(dev, (dev + 1) % 8) for dev in range(8)])  83.5 us
    reduce_scatter x1, waiting for transfers between devices, shards(): lax.psum_scatter(outputs.astype(jnp.bfloat16), 'tensor', scatter_dimensio...  60.2 us
    all_to_all x1, blocking collectives, trade(): lax.all_to_all(buffer, 'expert', split_axis=0, concat_axis=0, tiled=True)  25.6 us
    all_to_all x1, waiting for transfers between devices, trade(): lax.all_to_all(buffer, 'expert', split_axis=0, concat_axis=0, tiled=True)  16.9 us
    dot_general x1, matrix products, add_up(): return jnp.dot(normed, piece, preferred_element_type=jnp.float32)  9.65 us
    dot_general x1, matrix products, add_down(): lax.dot_general(ffn_active, piece, (((1,), (1,)), ((), ())), preferred_el...  9.55 us
    unnamed x24, local copies, waits for them, and re-layouts  8.16 us
  transfers between devices with their start and end apart: 12, of which 10 were waited for; matrix products, arithmetic and copies ran while one was open for 6% of the time, Pallas kernels for 0%

profile of v1, /device:TPU:1, one launch (start us, length us, event | category | flops | bytes accessed | tf_op | source)
XLA Modules:
  0.0 365.6 jit_solution(17387874426519163362)
XLA Ops:
  7.4 1.0 convert_reduce_fusion
  8.4 0.7 multiply_add_fusion
  9.1 1.8 fusion.27
  10.8 25.6 %all_to_all.10 = bf16[32,2,16,512]{3,2,1,0:T(8,128)(2,1)S(1)} all-to-all(bf16[32,2,16,512]{3,2,1,0:T(8,128)(2,1)S(1)} %bitcast.30), channel_id=1, replica_groups=mesh['expert'=32,'tensor'=8] {'expert'}, dimensions={0} | all-to-all | bytes 2097152 | tf_op jit(solution)/shard_map/all_to_all | solution.py:21
  36.4 6.6 %convert_bitcast_fusion = bf16[32,2,16,2048]{3,2,0,1:T(8,128)(2,1)} fusion(bf16[2,512,2048]{2,1,0:T(8,128)(2,1)} %param.11, bf16[32,2,16,512]{3,2,1,0:T(8,128)(2,1)S(1)} %all_to_all.10), kind=kOutput, calls=%fused_computation.15 | convolution fusion | flops 2149580800 | bytes 9437184 | tf_op jit(solution)/shard_map/sjcd,jdh->sjch/dot_general | solution.py:39
  43.0 0.0 all-reduce.2.cloned.1.call-update
  43.0 0.0 all-gather.3.cloned.1.call-start
  43.0 0.5 all-gather.3.cloned.1.call-update
  43.6 0.0 all-gather.5.cloned.1.call-start
  43.6 0.5 all-gather.5.cloned.1.call-update
  44.2 0.0 copy-start.1
  44.2 0.0 copy-start.3
  44.2 106.9 %all-reduce.2.cloned.1.call-done = bf16[32,2,16,2048]{3,2,0,1:T(8,128)(2,1)} async-done(((bf16[32,2,16,2048]{3,2,0,1:T(8,128)(2,1)}), bf16[32,2,16,2048]{3,2,0,1:T(8,128)(2,1)}) %all-reduce.2.cloned.1.call-update) | async-done | bytes 4194320 | tf_op jit(solution)/shard_map/psum | solution.py:42
  151.1 6.1 %fusion.31 = bf16[32,2,16,512]{3,2,0,1:T(8,128)(2,1)S(1)} fusion(bf16[2,2048,512]{2,1,0:T(8,128)(2,1)} %param.12, bf16[32,2,16,2048]{3,2,0,1:T(8,128)(2,1)} %all-reduce.2.cloned.1.call-done), kind=kOutput, calls=%fused_computation.31 | convolution fusion | flops 2154299392 | bytes 9437184 | tf_op jit(solution)/shard_map/sjch,jhd->sjcd/dot_general | solution.py:44
  157.2 1.0 copy.28
  158.3 7.5 %all-to-all-start.1 = ((bf16[32,2,16,512]{3,2,1,0:T(8,128)(2,1)}), bf16[32,2,16,512]{3,2,1,0:T(8,128)(2,1)S(1)}, u32[]{:S(2)}, u32[]{:S(2)}) async-start(bf16[32,2,16,512]{3,2,1,0:T(8,128)(2,1)} %copy.28), calls=%async_computation.1 | async-start | bytes 2097152 | tf_op jit(solution)/shard_map/all_to_all | solution.py:21
  165.8 0.0 reduce-scatter.2.cloned.1.call-start
  165.9 0.2 copy.26
  166.1 16.9 %all-to-all-done.1 = bf16[32,2,16,512]{3,2,1,0:T(8,128)(2,1)S(1)} async-done(((bf16[32,2,16,512]{3,2,1,0:T(8,128)(2,1)}), bf16[32,2,16,512]{3,2,1,0:T(8,128)(2,1)S(1)}, u32[]{:S(2)}, u32[]{:S(2)}) %all-to-all-start.1) | async-done | bytes 1048608 | tf_op jit(solution)/shard_map/all_to_all | solution.py:21
  183.0 0.8 fusion.36
  183.8 0.1 collective-permute-start
  183.9 14.3 %collective-permute-done = bf16[512,512]{0,1:T(8,128)(2,1)S(1)} collective-permute-done((bf16[512,512]{0,1:T(8,128)(2,1)S(1)}, bf16[512,512]{0,1:T(8,128)(2,1)S(1)}, u32[]{:S(2)}, u32[]{:S(2)}) %collective-permute-start) | collective-permute-done | bytes 524320 | tf_op jit(solution)/shard_map/ppermute | solution.py:54
  198.2 0.0 collective-permute-start.1
  198.2 13.4 %collective-permute-done.1 = bf16[512,512]{0,1:T(8,128)(2,1)S(1)} collective-permute-done((bf16[512,512]{0,1:T(8,128)(2,1)S(1)}, bf16[512,512]{0,1:T(8,128)(2,1)S(1)}, u32[]{:S(2)}, u32[]{:S(2)}) %collective-permute-start.1) | collective-permute-done | bytes 524320 | tf_op jit(solution)/shard_map/ppermute | solution.py:54
  211.6 0.0 collective-permute-start.2
  211.6 12.5 %collective-permute-done.2 = bf16[512,512]{0,1:T(8,128)(2,1)S(1)} collective-permute-done((bf16[512,512]{0,1:T(8,128)(2,1)S(1)}, bf16[512,512]{0,1:T(8,128)(2,1)S(1)}, u32[]{:S(2)}, u32[]{:S(2)}) %collective-permute-start.2) | collective-permute-done | bytes 524320 | tf_op jit(solution)/shard_map/ppermute | solution.py:54
  224.1 11.6 %collective-permute-done.3 = bf16[512,512]{0,1:T(8,128)(2,1)S(1)} collective-permute-done((bf16[512,512]{0,1:T(8,128)(2,1)S(1)}, bf16[512,512]{0,1:T(8,128)(2,1)S(1)}, u32[]{:S(2)}, u32[]{:S(2)}) %collective-permute-start.3) | collective-permute-done | bytes 524320 | tf_op jit(solution)/shard_map/ppermute | solution.py:54
  235.6 0.0 collective-permute-start.4
  235.6 10.6 %collective-permute-done.4 = bf16[512,512]{0,1:T(8,128)(2,1)S(1)} collective-permute-done((bf16[512,512]{0,1:T(8,128)(2,1)S(1)}, bf16[512,512]{0,1:T(8,128)(2,1)S(1)}, u32[]{:S(2)}, u32[]{:S(2)}) %collective-permute-start.4) | collective-permute-done | bytes 524320 | tf_op jit(solution)/shard_map/ppermute | solution.py:54
  246.3 0.0 collective-permute-start.5
  246.3 10.5 %collective-permute-done.5 = bf16[512,512]{0,1:T(8,128)(2,1)} collective-permute-done((bf16[512,512]{0,1:T(8,128)(2,1)S(1)}, bf16[512,512]{0,1:T(8,128)(2,1)}, u32[]{:S(2)}, u32[]{:S(2)}) %collective-permute-start.5) | collective-permute-done | bytes 524320 | tf_op jit(solution)/shard_map/ppermute | solution.py:54
  256.7 0.0 collective-permute-start.6
  256.8 10.7 %collective-permute-done.6 = bf16[512,512]{0,1:T(8,128)(2,1)} collective-permute-done((bf16[512,512]{0,1:T(8,128)(2,1)}, bf16[512,512]{0,1:T(8,128)(2,1)}, u32[]{:S(2)}, u32[]{:S(2)}) %collective-permute-start.6) | collective-permute-done | bytes 524320 | tf_op jit(solution)/shard_map/ppermute | solution.py:54
  267.4 1.1 constant_dynamic-update-slice_fusion.15
  268.5 1.1 constant_dynamic-update-slice_fusion.14
  269.7 0.0 copy-start.2
  269.9 1.1 constant_dynamic-update-slice_fusion.7
  271.0 1.1 constant_dynamic-update-slice_fusion.6
  272.3 3.2 copy-done
  275.5 0.9 fusion
  276.5 0.0 all-gather.3.cloned.1.call-done
  276.5 9.6 %fusion.22 = bf16[512,1024]{1,0:T(8,128)(2,1)S(1)} fusion(bf16[4096,1024]{1,0:T(8,128)(2,1)} %all-gather.3.cloned.1.call-done, f32[4096]{0:T(1024)S(1)} %copy-done.2, f32[512]{0:T(512)S(1)} %add_rsqrt_fusion, bf16[512,8192]{0,1:T(8,128)(2,1)} %copy-done, s32[]{:T(128)S(6)} %select_n.14), kind=kOutput, calls=%fused_computation.25 | convolution fusion | flops 4308074496 | bytes 13649924 | tf_op jit(solution)/shard_map/dot_general | solution.py:65
  286.2 0.0 all-gather.5.cloned.1.call-done
  286.2 9.5 %convolution_convert_fusion = bf16[512,4096]{0,1:T(8,128)(2,1)} fusion(bf16[512,1024]{1,0:T(8,128)(2,1)S(1)} %fusion.22, bf16[4096,1024]{1,0:T(8,128)(2,1)} %all-gather.5.cloned.1.call-done), kind=kOutput, calls=%fused_computation.6 | convolution fusion | flops 4297064448 | bytes 13631488 | tf_op jit(solution)/shard_map/dot_general | solution.py:73
  295.8 0.0 reduce-scatter.2.cloned.1.call-update
  295.8 60.2 %reduce-scatter.2.cloned.1.call-done = bf16[512,512]{0,1:T(8,128)(2,1)} async-done(((bf16[512,4096]{0,1:T(8,128)(2,1)}), bf16[512,512]{0,1:T(8,128)(2,1)}) %reduce-scatter.2.cloned.1.call-update) | async-done | bytes 524304 | tf_op jit(solution)/shard_map/reduce_scatter | solution.py:81
  356.0 1.2 add_convert_fusion
  357.2 1.0 copy.30
  (19 shorter events, 0.5 us)
Async XLA Ops:
  7.4 143.7 %all-reduce.2.cloned.1.call-start = ((), (), s32[]{:S(2)}) async-start(), calls=%async_computation.3 | async-start | bytes 8388608 | tf_op jit(solution)/shard_map/psum | solution.py:42
  43.0 233.5 %all-gather.3.cloned.1.call-start = ((), (), s32[]{:S(2)}) async-start(), calls=%async_computation.4 | async-start | bytes 8650752 | tf_op jit(solution)/shard_map/all_gather | solution.py:26
  43.6 242.6 %all-gather.5.cloned.1.call-start = ((), (), s32[]{:S(2)}) async-start(), calls=%async_computation.5 | async-start | bytes 8650752 | tf_op jit(solution)/shard_map/all_gather | solution.py:26
  44.2 121.7 %copy-start.1 = (bf16[512,512]{1,0:T(8,128)(2,1)S(1)}, bf16[512,512]{1,0:T(8,128)(2,1)}, u32[]{:S(2)}) copy-start(bf16[512,512]{1,0:T(8,128)(2,1)} %param.8) | copy-start | bytes 1572868
  44.2 138.8 %copy-start.3 = (f32[512,1]{0,1:T(1,128)S(1)}, f32[512,1]{0,1:T(1,128)}, u32[]{:S(2)}) copy-start(f32[512,1]{0,1:T(1,128)} %param.10) | copy-start | bytes 6148
  158.3 24.7 %all-to-all-start.1 = ((bf16[32,2,16,512]{3,2,1,0:T(8,128)(2,1)}), bf16[32,2,16,512]{3,2,1,0:T(8,128)(2,1)S(1)}, u32[]{:S(2)}, u32[]{:S(2)}) async-start(bf16[32,2,16,512]{3,2,1,0:T(8,128)(2,1)} %copy.28), calls=%async_computation.1 | async-start | bytes 2097152 | tf_op jit(solution)/shard_map/all_to_all | solution.py:21
  165.8 190.2 %reduce-scatter.2.cloned.1.call-start = ((), (), s32[]{:S(2)}) async-start(), calls=%async_computation.6 | async-start | bytes 4718592 | tf_op jit(solution)/shard_map/reduce_scatter | solution.py:81
  183.8 14.4 %collective-permute-start = (bf16[512,512]{0,1:T(8,128)(2,1)S(1)}, bf16[512,512]{0,1:T(8,128)(2,1)S(1)}, u32[]{:S(2)}, u32[]{:S(2)}) collective-permute-start(bf16[512,512]{0,1:T(8,128)(2,1)S(1)} %fusion.36), channel_id=1, source_target_pairs={{0,1},{1,2},{2,3},{3,4},{4,5},{5,6},{6,7},{7,0},{8,9},{9,10},{10,1... | collective-permute-start | bytes 1572872 | tf_op jit(solution)/shard_map/ppermute | solution.py:54
  198.2 13.4 %collective-permute-start.1 = (bf16[512,512]{0,1:T(8,128)(2,1)S(1)}, bf16[512,512]{0,1:T(8,128)(2,1)S(1)}, u32[]{:S(2)}, u32[]{:S(2)}) collective-permute-start(bf16[512,512]{0,1:T(8,128)(2,1)S(1)} %collective-permute-done), channel_id=1, source_target_pairs={{0,1},{1,2},{2,3},{3,4},{4,5},{5,6},{6,7},{7,0},{8,9},{9,10},{10,1... | collective-permute-start | bytes 1572872 | tf_op jit(solution)/shard_map/ppermute | solution.py:54
  211.6 12.5 %collective-permute-start.2 = (bf16[512,512]{0,1:T(8,128)(2,1)S(1)}, bf16[512,512]{0,1:T(8,128)(2,1)S(1)}, u32[]{:S(2)}, u32[]{:S(2)}) collective-permute-start(bf16[512,512]{0,1:T(8,128)(2,1)S(1)} %collective-permute-done.1), channel_id=1, source_target_pairs={{0,1},{1,2},{2,3},{3,4},{4,5},{5,6},{6,7},{7,0},{8,9},{9,10},{10,1... | collective-permute-start | bytes 1572872 | tf_op jit(solution)/shard_map/ppermute | solution.py:54
  224.1 11.6 %collective-permute-start.3 = (bf16[512,512]{0,1:T(8,128)(2,1)S(1)}, bf16[512,512]{0,1:T(8,128)(2,1)S(1)}, u32[]{:S(2)}, u32[]{:S(2)}) collective-permute-start(bf16[512,512]{0,1:T(8,128)(2,1)S(1)} %collective-permute-done.2), channel_id=1, source_target_pairs={{0,1},{1,2},{2,3},{3,4},{4,5},{5,6},{6,7},{7,0},{8,9},{9,10},{10,1... | collective-permute-start | bytes 1572872 | tf_op jit(solution)/shard_map/ppermute | solution.py:54
  235.6 10.6 %collective-permute-start.4 = (bf16[512,512]{0,1:T(8,128)(2,1)S(1)}, bf16[512,512]{0,1:T(8,128)(2,1)S(1)}, u32[]{:S(2)}, u32[]{:S(2)}) collective-permute-start(bf16[512,512]{0,1:T(8,128)(2,1)S(1)} %collective-permute-done.3), channel_id=1, source_target_pairs={{0,1},{1,2},{2,3},{3,4},{4,5},{5,6},{6,7},{7,0},{8,9},{9,10},{10,1... | collective-permute-start | bytes 1572872 | tf_op jit(solution)/shard_map/ppermute | solution.py:54
  246.3 10.5 %collective-permute-start.5 = (bf16[512,512]{0,1:T(8,128)(2,1)S(1)}, bf16[512,512]{0,1:T(8,128)(2,1)}, u32[]{:S(2)}, u32[]{:S(2)}) collective-permute-start(bf16[512,512]{0,1:T(8,128)(2,1)S(1)} %collective-permute-done.4), channel_id=1, source_target_pairs={{0,1},{1,2},{2,3},{3,4},{4,5},{5,6},{6,7},{7,0},{8,9},{9,10},{10,1... | collective-permute-start | bytes 1572872 | tf_op jit(solution)/shard_map/ppermute | solution.py:54
  256.7 10.7 %collective-permute-start.6 = (bf16[512,512]{0,1:T(8,128)(2,1)}, bf16[512,512]{0,1:T(8,128)(2,1)}, u32[]{:S(2)}, u32[]{:S(2)}) collective-permute-start(bf16[512,512]{0,1:T(8,128)(2,1)} %collective-permute-done.5), channel_id=1, source_target_pairs={{0,1},{1,2},{2,3},{3,4},{4,5},{5,6},{6,7},{7,0},{8,9},{9,10},{10,1... | collective-permute-start | bytes 1572872 | tf_op jit(solution)/shard_map/ppermute | solution.py:54
  269.7 6.8 %copy-start.2 = (f32[4096]{0:T(1024)S(1)}, f32[4096]{0:T(1024)}, u32[]{:S(2)}) copy-start(f32[4096]{0:T(1024)} %param.13) | copy-start | bytes 49156
  272.3 3.2 copy-start
Sparse Core Ops, SparseCore 0:
  43.1 107.9 all-reduce.1
  295.9 60.0 reduce-scatter.1
Sparse Core Ops, SparseCore 1:
  46.0 57.1 all-gather.2
  105.6 57.4 all-gather.4
